TPU v7x, 512 devices: a whole 4x8x8 slice. The times are simulated.
512 devices in a mesh: mp: 8 (over z_hi, core), feat: 64 (over z_lo, x, y).
Axes of the slice: x: 4, y: 8, z: 8 (z_hi: 4, z_lo: 2; z = z_hi * 2 + z_lo), core: 2. Of those that a mesh axis runs over, the one named last changes fastest.
Arguments:
- residual: bfloat16 [2, 384, 2304], P(None, 'feat', 'mp'), may hold values from -6 to 6
- norm_gain: float32 [2, 2304], P(None, 'mp'), may hold values from 0.1 to 1.9
- gate_weight: bfloat16 [2, 2304, 9216], P(None, 'mp', 'feat'), may hold values from -0.125 to 0.125
- up_weight: bfloat16 [2, 2304, 9216], P(None, 'mp', 'feat'), may hold values from -0.125 to 0.125
- down_weight: bfloat16 [2, 9216, 2304], P(None, 'feat', 'mp'), may hold values from -0.0625 to 0.0625
- encoder: bfloat16 [2, 32768, 2304], P(None, 'feat', 'mp'), may hold values from -0.125 to 0.125
- encoder_bias: float32 [2, 32768], P(None, 'feat'), may hold values from -3 to 3
- decoder: bfloat16 [3, 32768, 2304], P(None, 'feat', 'mp'), may hold values from -0.03125 to 0.03125
Outputs:
- grad_encoder: bfloat16 [2, 32768, 2304], P(None, 'feat', 'mp')
- grad_bias: float32 [2, 32768], P(None, 'feat')
- grad_decoder: bfloat16 [3, 32768, 2304], P(None, 'feat', 'mp')
All inputs are finite; a program needn't handle non-finite values.
Results may differ from a plain program's by a relative error of at most 0.02.
The roundings to bfloat16 on the way count: a program that leaves them out, or rounds other values in their place, can miss the bound.
Values may be sent and summed in bfloat16 or wider, within the bound.
A program may use at most 64 MiB of HBM per device.

v0:
```python
import math

import jax
import jax.numpy as jnp
from jax import lax
from jax.sharding import PartitionSpec as P

D = 2304


sparsity_weight = 0.1


def outer_product(weights_side, errors_side):
    return lax.dot_general(
        weights_side, errors_side, (((0,), (0,)), ((), ())), preferred_element_type=jnp.float32
    )


def body(residual, norm_gain, gate_weight, up_weight, down_weight, encoder, encoder_bias, decoder):
    values = residual.astype(jnp.float32)
    squares = lax.psum(jnp.sum(values * values, axis=2), "mp")
    inverse_rms = lax.rsqrt(squares / D + 1e-06)
    normed_local = (values * inverse_rms[:, :, None] * norm_gain[:, None, :]).astype(jnp.bfloat16)
    normed = lax.all_gather(normed_local, "feat", axis=1, tiled=True)
    tokens = normed.shape[1]
    local_rows = residual.shape[1]
    gate_part = jnp.einsum("ltd,ldh->lth", normed, gate_weight, preferred_element_type=jnp.float32)
    up_part = jnp.einsum("ltd,ldh->lth", normed, up_weight, preferred_element_type=jnp.float32)
    gate_part, up_part = (
        lax.psum(gate_part.astype(jnp.bfloat16), "mp").astype(jnp.float32),
        lax.psum(up_part.astype(jnp.bfloat16), "mp").astype(jnp.float32),
    )
    hidden = (jax.nn.gelu(gate_part, approximate=True) * up_part).astype(jnp.bfloat16)
    preact_part = jnp.einsum("ltd,lfd->tlf", normed, encoder, preferred_element_type=jnp.float32)
    preact = lax.psum(preact_part, "mp")
    active = jnp.maximum(preact + encoder_bias[None], 0.0).astype(jnp.bfloat16)
    features = active.shape[2]
    model_cols = decoder.shape[2]
    joined = jnp.concatenate([decoder[1], decoder[2]], axis=0)
    picked = hidden
    partial_value = jnp.einsum(
        "lth,lhd->tld", picked, down_weight, preferred_element_type=jnp.float32
    )
    target = lax.psum_scatter(
        partial_value.reshape(local_rows * lax.axis_size("feat"), -1),
        "feat",
        scatter_dimension=0,
        tiled=True,
    )
    picked = active
    first_part = jnp.dot(picked[:, 0], decoder[0], preferred_element_type=jnp.float32)
    second = jnp.dot(
        picked.reshape(local_rows * lax.axis_size("feat"), 2 * features),
        joined,
        preferred_element_type=jnp.float32,
    )
    rebuilt = lax.psum_scatter(
        jnp.concatenate([first_part, second], axis=1), "feat", scatter_dimension=0, tiled=True
    )
    errors_local = (rebuilt - target).astype(jnp.bfloat16)
    errors = lax.all_gather(errors_local, "feat", axis=0, tiled=True)
    error_first = errors[:, :model_cols]
    error_second = errors[:, model_cols:]
    first_rows = jnp.concatenate([decoder[0], decoder[1]], axis=1)
    back_first = lax.dot_general(
        errors, first_rows, (((1,), (1,)), ((), ())), preferred_element_type=jnp.float32
    )
    back_second = lax.dot_general(
        error_second, decoder[2], (((1,), (1,)), ((), ())), preferred_element_type=jnp.float32
    )
    back_stack = jnp.stack([back_first, back_second], axis=1)
    loss_scale = 1.0 / math.sqrt(tokens)
    backward = lax.psum(back_stack.astype(jnp.bfloat16), "mp").astype(jnp.float32)
    pre_grad = jnp.where(active > 0, loss_scale * (backward + sparsity_weight), 0.0).astype(
        jnp.bfloat16
    )
    grad_encoder = jnp.einsum(
        "tlf,ltd->lfd", pre_grad, normed, preferred_element_type=jnp.float32
    ).astype(jnp.bfloat16)
    grad_bias = jnp.sum(pre_grad.astype(jnp.float32), axis=0)
    active_first = active[:, 0]
    active_second = active[:, 1]
    grad_decoder = (
        loss_scale
        * jnp.stack(
            [
                outer_product(active_first, error_first),
                outer_product(active_first, error_second),
                outer_product(active_second, error_second),
            ]
        )
    ).astype(jnp.bfloat16)
    return (grad_encoder, grad_bias, grad_decoder)


def solution(mesh):
    return jax.shard_map(
        body,
        mesh=mesh,
        in_specs=(
            P(None, "feat", "mp"),
            P(None, "mp"),
            P(None, "mp", "feat"),
            P(None, "mp", "feat"),
            P(None, "feat", "mp"),
            P(None, "feat", "mp"),
            P(None, "feat"),
            P(None, "feat", "mp"),
        ),
        out_specs=(P(None, "feat", "mp"), P(None, "feat"), P(None, "feat", "mp")),
        check_vma=False,
    )
```

profile of v0, /device:TPU:1, one launch (start us, length us, event | category | flops | bytes accessed | tf_op | source)
XLA Modules:
  0.0 1201.5 jit_solution(16398808763718238161)
XLA Ops:
  7.2 0.9 fusion.34
  8.1 20.4 %psum.35 = f32[2,6]{0,1:T(8,128)S(1)} all-reduce(f32[2,6]{0,1:T(8,128)S(1)} %fusion.34), channel_id=1, replica_groups=mesh['mp'=8,'feat'=64] {'mp'}, use_global_device_ids=true, to_apply=%region_1.0 | all-reduce | flops 12 | bytes 96 | tf_op jit(solution)/shard_map/psum | solution.py:22
  29.4 131.8 %all_gather.6 = bf16[2,384,288]{2,0,1:T(2,128)(2,1)S(1)} all-gather(bf16[2,6,288]{2,0,1:T(2,128)(2,1)S(1)} %fusion.36), channel_id=1, replica_groups=mesh['mp'=8,'feat'=64] {'feat'}, dimensions={1}, use_global_device_ids=true | all-gather | bytes 449280 | tf_op jit(solution)/shard_map/all_gather | solution.py:25
  161.2 2.0 convolution_convert_fusion.3
  163.1 1.0 convolution_convert_fusion.4
  164.2 1.7 convolution_bitcast_fusion
  166.9 95.3 %all-reduce.15.cloned.1.call-done = (bf16[2,384,144]{1,2,0:T(8,128)(2,1)}, bf16[2,384,144]{1,2,0:T(8,128)(2,1)}) async-done(((bf16[2,384,144]{1,2,0:T(8,128)(2,1)}, bf16[2,384,144]{1,2,0:T(8,128)(2,1)}), (bf16[2,384,144]{1,2,0:T(8,128)(2,1)}, bf16[2,384,144]{1,2,0:T(8,128)(2,1)})) %all-reduce.15.cloned.1.call-update) | async-done | bytes 442384 | tf_op jit(solution)/shard_map/psum | solution.py:31
  262.3 2.4 fusion.27
  264.7 85.0 %all-reduce.9.cloned.1.call-done = f32[384,2,512]{2,0,1:T(8,128)} async-done(((f32[384,2,512]{2,0,1:T(8,128)}), f32[384,2,512]{2,0,1:T(8,128)}) %all-reduce.9.cloned.1.call-update) | async-done | bytes 1572880 | tf_op jit(solution)/shard_map/psum | solution.py:36
  349.7 1.6 maximum_convert_fusion
  351.3 1.2 copy.16
  352.8 1.8 fusion.3
  354.6 1.0 pad_maximum_fusion
  355.7 1.3 dynamic-slice
  357.6 554.6 %all-reduce.13.cloned.1.call-done = (f32[384,576]{0,1:T(8,128)}, f32[384,576]{0,1:T(8,128)}) async-done(((f32[384,576]{0,1:T(8,128)}, f32[384,576]{0,1:T(8,128)}), (f32[384,576]{0,1:T(8,128)}, f32[384,576]{0,1:T(8,128)})) %all-reduce.13.cloned.1.call-update) | async-done | bytes 1769488
  912.2 1.5 fusion.33
  913.8 131.7 %all-gather = bf16[64,6,576]{2,1,0:T(8,128)(2,1)S(1)} all-gather(bf16[1,6,576]{2,1,0:T(8,128)(2,1)S(1)} %copy.19), channel_id=1, replica_groups=mesh['mp'=8,'feat'=64] {'feat'}, dimensions={0}, use_global_device_ids=true | all-gather | bytes 449280 | tf_op jit(solution)/shard_map/all_gather | solution.py:62
  1045.8 1.4 fusion.1
  1047.1 1.4 fusion.2
  1048.6 1.0 pad_maximum_fusion.1
  1051.2 1.2 fusion
  1052.3 139.0 %all-reduce.11.cloned.1.call-done = bf16[384,2,512]{2,0,1:T(8,128)(2,1)} async-done(((bf16[384,2,512]{2,0,1:T(8,128)(2,1)}), bf16[384,2,512]{2,0,1:T(8,128)(2,1)}) %all-reduce.11.cloned.1.call-update) | async-done | bytes 786448 | tf_op jit(solution)/shard_map/psum | solution.py:74
  1191.3 2.2 convert_reduce_fusion
  1193.5 1.4 convolution_convert_fusion
  (31 shorter events, 4.2 us)
Async XLA Ops:
  7.2 157.1 %copy-start = (bf16[2,512,288]{1,2,0:T(8,128)(2,1)S(1)}, bf16[2,512,288]{1,2,0:T(8,128)(2,1)}, u32[]{:S(2)}) copy-start(bf16[2,512,288]{1,2,0:T(8,128)(2,1)} %param.13) | copy-start | bytes 1769476
  7.2 155.9 %copy-start.5 = (bf16[2,288,144]{1,2,0:T(8,128)(2,1)S(1)}, bf16[2,288,144]{1,2,0:T(8,128)(2,1)}, u32[]{:S(2)}) copy-start(bf16[2,288,144]{1,2,0:T(8,128)(2,1)} %param.10) | copy-start | bytes 497668
  7.2 255.1 %all-reduce.15.cloned.1.call-start = ((), (), s32[]{:S(2)}) async-start(), calls=%async_computation.3 | async-start | bytes 884736 | tf_op jit(solution)/shard_map/psum | solution.py:31
  164.2 1.9 copy-start.2
  164.2 185.5 %all-reduce.9.cloned.1.call-start = ((), (), s32[]{:S(2)}) async-start(), calls=%async_computation | async-start | bytes 3145728 | tf_op jit(solution)/shard_map/psum | solution.py:36
  166.0 96.3 %copy-start.6 = (bf16[2,144,288]{2,1,0:T(8,128)(2,1)S(1)}, bf16[2,144,288]{2,1,0:T(8,128)(2,1)}, u32[]{:S(2)}) copy-start(bf16[2,144,288]{2,1,0:T(8,128)(2,1)} %param.12) | copy-start | bytes 497668
  166.0 183.7 %copy-start.4 = (f32[2,512]{1,0:T(2,128)S(1)}, f32[2,512]{1,0:T(2,128)}, u32[]{:S(2)}) copy-start(f32[2,512]{1,0:T(2,128)} %param.14) | copy-start | bytes 12292
  166.0 746.2 %all-reduce.13.cloned.1.call-start = ((), (), s32[]{:S(2)}) async-start(), calls=%async_computation.2 | async-start | bytes 3538944
  355.6 835.7 %all-reduce.11.cloned.1.call-start = ((), (), s32[]{:S(2)}) async-start(), calls=%async_computation.1 | async-start | bytes 1572864 | tf_op jit(solution)/shard_map/psum | solution.py:74
  1051.2 140.1 %copy-start.1 = (f32[384,2,512]{2,0,1:T(8,128)S(1)}, f32[384,2,512]{2,0,1:T(8,128)}, u32[]{:S(2)}) copy-start(f32[384,2,512]{2,0,1:T(8,128)} %all-reduce.9.cloned.1.call-done) | copy-start | bytes 4718596
  1191.3 2.2 copy-start.3
Sparse Core Ops, SparseCore 0:
  164.3 97.9 all-reduce.14
  265.5 84.1 all-reduce.8
  355.7 556.4 all-reduce.12
  1049.7 141.5 all-reduce.10
where the time goes:
time: 1200 us
  waiting for transfers between devices  874 us (73%)
  blocking collectives  284 us (24%)
  matrix products  15.1 us (1%)
  between operations  14.5 us (1%)
    unnamed x5, waiting for transfers between devices  555 us
    psum x1, waiting for transfers between devices, body(): lax.psum(back_stack.astype(jnp.bfloat16), 'mp').astype(jnp.float32)  139 us
    all_gather x1, blocking collectives, body(): normed = lax.all_gather(normed_local, 'feat', axis=1, tiled=True)  132 us
    all_gather x1, blocking collectives, body(): errors = lax.all_gather(errors_local, 'feat', axis=0, tiled=True)  132 us
    psum x1, waiting for transfers between devices, body(): lax.psum(gate_part.astype(jnp.bfloat16), 'mp').astype(jnp.float32)  95.3 us
    psum x1, waiting for transfers between devices, body(): preact = lax.psum(preact_part, 'mp')  85 us
  transfers between devices with their start and end apart: 4, of which 4 were waited for; matrix products, arithmetic and copies ran while one was open for 1% of the time, Pallas kernels for 0%

commit v1 on v0

v1 whole, which is shorter than its diff:
```python
import functools
import math

import jax
import jax.numpy as jnp
from jax import lax
from jax.experimental import pallas as pl
from jax.experimental.pallas import tpu as pltpu
from jax.sharding import PartitionSpec as P

MESH = pl.DeviceIdType.MESH
F32 = jnp.float32
BF16 = jnp.bfloat16
sparsity_weight = 0.1

STAGE_TIMES = (0, 2, 8, 13, 15, 20, 25, 30, 32, 37, 42, 44)
CHUNK_STEP = 9.0


def nt(a, b):
    return lax.dot_general(a, b, (((1,), (1,)), ((), ())), preferred_element_type=F32)


def tn(a, b):
    return lax.dot_general(a, b, (((0,), (0,)), ((), ())), preferred_element_type=F32)


def kernel(
    width, residual, gain, gate_w, up_w, down_w, encoder, bias, decoder,
    grad_encoder, grad_bias, grad_decoder,
    squares, padded, xl_block, own_block, normed, w_dec, w_enc, w_gate,
    pre_mine, pre_core, pre_z, pre_recv, gu_mine, gu_core, gu_z, gu_recv,
    act, err_part, err_recv, err_xl, errors, mask,
    back_mine, back_core, back_z, back_recv, grads, enc_sum,
    sems,
):
    layers, local, cols = residual.shape
    feats = encoder.shape[1]
    hid = gate_w.shape[2]
    chunks, slots, rows, _ = normed.shape
    chunk_tokens = slots * rows
    both = layers * feats
    tokens = chunks * chunk_tokens
    scale = 1.0 / math.sqrt(tokens)

    mp = lax.axis_index("mp")
    ft = lax.axis_index("feat")
    zh, core = mp // 2, mp % 2
    xl, yy = ft // 8, ft % 8
    mine = core * 4 + zh

    core_dev = (zh * 2 + 1 - core, ft)
    z_at = [(zh + d) % 4 for d in (1, 2, 3)]
    z_dev = [(z * 2 + core, ft) for z in z_at]
    far_dev = [(z * 2 + 1 - core, ft) for z in z_at]
    xl_at = [(xl + d) % 8 for d in range(1, 8)]
    xl_dev = [(mp, a * 8 + yy) for a in xl_at]
    y_at = [(yy + d) % 8 for d in range(1, 8)]
    y_dev = [(mp, xl * 8 + a) for a in y_at]
    partners = [core_dev] + z_dev + far_dev + xl_dev + y_dev

    pending = []

    def send(i, src, dst, dev):
        pltpu.make_async_remote_copy(
            src_ref=src, dst_ref=dst, send_sem=sems.at[0, i], recv_sem=sems.at[1, i],
            device_id=dev, device_id_type=MESH,
        ).start()

    def wait(side, i, ref):
        pltpu.make_async_copy(ref, ref, sems.at[side, i]).wait()

    barrier = pltpu.get_barrier_semaphore()
    for dev in partners:
        pl.semaphore_signal(barrier, inc=1, device_id=dev, device_id_type=MESH)

    values = [residual[l].astype(F32) for l in range(layers)]
    for l in range(layers):
        total = jnp.sum(values[l] * values[l], axis=1, keepdims=True)
        squares[mp, l] = jnp.zeros((8, 128), F32)
        squares[mp, l, 0:local, :] = jnp.broadcast_to(total, (local, 128))
    padded[...] = jnp.zeros_like(padded)

    pl.semaphore_wait(barrier, len(partners))

    for dev in z_dev + far_dev + [core_dev]:
        send(0, squares.at[mp], squares.at[mp], dev)
    pending.append((0, squares.at[0:7]))

    w_dec[...] = jnp.zeros_like(w_dec)
    w_dec[0:feats, 0:cols] = decoder[0]
    w_dec[0:feats, cols : 2 * cols] = decoder[1]
    w_dec[feats:both, cols : 2 * cols] = decoder[2]
    w_dec[both : both + hid, 0:cols] = down_w[0]
    w_dec[both + hid : both + 2 * hid, cols : 2 * cols] = down_w[1]
    w_enc[...] = jnp.zeros_like(w_enc)
    w_enc[0:feats, 0:cols] = encoder[0]
    w_enc[feats:both, cols : 2 * cols] = encoder[1]
    up_at = gu_mine.shape[3] - 2 * hid
    w_gate[...] = jnp.zeros_like(w_gate)
    for l in range(layers):
        w_gate[l * cols : (l + 1) * cols, l * hid : (l + 1) * hid] = gate_w[l]
        w_gate[l * cols : (l + 1) * cols, up_at + l * hid : up_at + (l + 1) * hid] = up_w[l]

    wait(1, 0, squares.at[0:7])
    for l in range(layers):
        total = squares[0, l]
        for m in range(1, 8):
            total = total + squares[m, l]
        inverse = lax.rsqrt(total[0:local, 0:1] / width + 1e-06)
        padded[0:local, l * cols : (l + 1) * cols] = values[l] * inverse * gain[l : l + 1, :]
    xl_block[xl] = padded[...].astype(BF16)
    for dev in xl_dev:
        send(1, xl_block.at[xl], xl_block.at[xl], dev)
    pending.append((1, xl_block.at[0:7]))
    wait(1, 1, xl_block.at[0:7])
    for s in range(8):
        own_block[s * local : (s + 1) * local, :] = xl_block[s].astype(F32)[0:local, :]
    for k in range(chunks):
        normed[k, yy] = own_block[k * rows : (k + 1) * rows, :].astype(BF16)
        for dev in y_dev:
            send(2 + k, normed.at[k, yy], normed.at[k, yy], dev)
        pending.append((2 + k, normed.at[k, 0:7]))

    def slot(kind, k):
        return 2 + chunks * (1 + kind) + k

    def pre_matmul(k):
        wait(1, 2 + k, normed.at[k, 0:7])
        x = normed[k].reshape(chunk_tokens, 2 * cols)
        pre_mine[k] = nt(x, w_enc[...]).reshape(slots, rows, both)
        send(slot(0, k), pre_mine.at[k, pl.ds((1 - core) * 4, 4)], pre_core.at[k], core_dev)
        pending.append((slot(0, k), pre_core.at[k]))
        gu = jnp.dot(x, w_gate[...], preferred_element_type=F32)
        gu_mine[k] = gu.astype(BF16).reshape(slots, rows, -1)
        send(slot(1, k), gu_mine.at[k, pl.ds((1 - core) * 4, 4)], gu_core.at[k], core_dev)
        pending.append((slot(1, k), gu_core.at[k]))

    def pre_to_z(k):
        wait(1, slot(0, k), pre_core.at[k])
        for z, dev in zip(z_at, z_dev):
            pre_z[k, z] = pre_mine[k, core * 4 + z] + pre_core[k, z]
            send(slot(2, k), pre_z.at[k, z], pre_recv.at[k, zh], dev)
        pending.append((slot(2, k), pre_z.at[k, 0:3]))
        pre_recv[k, zh] = pre_mine[k, mine] + pre_core[k, zh]
        wait(1, slot(1, k), gu_core.at[k])
        for z, dev in zip(z_at, z_dev):
            gu_z[k, z] = (gu_mine[k, core * 4 + z].astype(F32) + gu_core[k, z].astype(F32)).astype(BF16)
            send(slot(3, k), gu_z.at[k, z], gu_recv.at[k, zh], dev)
        pending.append((slot(3, k), gu_z.at[k, 0:3]))
        gu_recv[k, zh] = (gu_mine[k, mine].astype(F32) + gu_core[k, zh].astype(F32)).astype(BF16)

    def activate(k):
        wait(1, slot(2, k), pre_recv.at[k, 0:3])
        total = pre_recv[k, 0] + pre_recv[k, 1] + pre_recv[k, 2] + pre_recv[k, 3]
        for l in range(layers):
            act[k, mine, :, l * feats : (l + 1) * feats] = jnp.maximum(
                total[:, l * feats : (l + 1) * feats] + bias[l : l + 1, :], 0.0
            ).astype(BF16)
        wait(1, slot(3, k), gu_recv.at[k, 0:3])
        gu = gu_recv[k, 0].astype(F32)
        for z in range(1, 4):
            gu = gu + gu_recv[k, z].astype(F32)
        hidden = jax.nn.gelu(gu[:, 0 : 2 * hid], approximate=True) * gu[:, up_at : up_at + 2 * hid]
        act[k, mine, :, both : both + 2 * hid] = -hidden.astype(BF16)
        for dev in z_dev:
            send(slot(4, k), act.at[k, mine], act.at[k, mine], dev)
        pending.append((slot(4, k), act.at[k, 0:3]))

    def act_to_core(k):
        wait(1, slot(4, k), act.at[k, 0:3])
        half = act.at[k, pl.ds(core * 4, 4)]
        send(slot(5, k), half, half, core_dev)
        pending.append((slot(5, k), act.at[k, 0:4]))

    def rebuild(k):
        wait(1, slot(5, k), act.at[k, 0:4])
        a = act[k].reshape(chunk_tokens, -1)
        err_part[k] = (
            jnp.dot(a, w_dec[...], preferred_element_type=F32).astype(BF16).reshape(slots, rows, -1)
        )
        for s, dev in zip(y_at, y_dev):
            send(slot(6, k), err_part.at[k, s], err_recv.at[k, yy], dev)
        pending.append((slot(6, k), err_part.at[k, 0:7]))
        err_recv[k, yy] = err_part[k, yy]
        start = pl.multiple_of(mine * 128, 128)
        own = act[k, :, :, pl.ds(start, 128)].reshape(chunk_tokens, 128)
        mask[k] = own.astype(F32).T

    def sum_y(k):
        wait(1, slot(6, k), err_recv.at[k, 0:7])
        total = err_recv[k, 0].astype(F32)
        for s in range(1, 8):
            total = total + err_recv[k, s].astype(F32)
        err_xl[k, xl] = total.astype(BF16)
        for dev in xl_dev:
            send(slot(7, k), err_xl.at[k, xl], err_xl.at[k, xl], dev)
        pending.append((slot(7, k), err_xl.at[k, 0:7]))

    def sum_xl(k):
        wait(1, slot(7, k), err_xl.at[k, 0:7])
        total = err_xl[k, 0].astype(F32)
        for s in range(1, 8):
            total = total + err_xl[k, s].astype(F32)
        errors[k, yy] = total.astype(BF16)
        for dev in y_dev:
            send(slot(8, k), errors.at[k, yy], errors.at[k, yy], dev)
        pending.append((slot(8, k), errors.at[k, 0:7]))

    def back_matmul(k):
        wait(1, slot(8, k), errors.at[k, 0:7])
        e = errors[k].reshape(chunk_tokens, 2 * cols)
        back = nt(w_dec[0:both, :], e)
        back_mine[k] = back.astype(BF16).reshape(slots, both // slots, chunk_tokens)
        send(slot(9, k), back_mine.at[k, pl.ds((1 - core) * 4, 4)], back_core.at[k], core_dev)
        pending.append((slot(9, k), back_core.at[k]))

    def back_to_z(k):
        wait(1, slot(9, k), back_core.at[k])
        for z, dev in zip(z_at, z_dev):
            back_z[k, z] = (
                back_mine[k, core * 4 + z].astype(F32) + back_core[k, z].astype(F32)
            ).astype(BF16)
            send(slot(10, k), back_z.at[k, z], back_recv.at[k, zh], dev)
        pending.append((slot(10, k), back_z.at[k, 0:3]))
        back_recv[k, zh] = (
            back_mine[k, mine].astype(F32) + back_core[k, zh].astype(F32)
        ).astype(BF16)

    def pre_grad(k):
        wait(1, slot(10, k), back_recv.at[k, 0:3])
        total = back_recv[k, 0].astype(F32)
        for z in range(1, 4):
            total = total + back_recv[k, z].astype(F32)
        grads[k, mine] = jnp.where(
            mask[k] > 0, scale * (total + sparsity_weight), 0.0
        ).astype(BF16)
        for dev in z_dev:
            send(slot(11, k), grads.at[k, mine], grads.at[k, mine], dev)
        pending.append((slot(11, k), grads.at[k, 0:3]))

    def grads_to_core(k):
        wait(1, slot(11, k), grads.at[k, 0:3])
        half = grads.at[k, pl.ds(core * 4, 4)]
        send(slot(12, k), half, half, core_dev)
        pending.append((slot(12, k), grads.at[k, 0:4]))

    def encoder_grads(k):
        wait(1, slot(12, k), grads.at[k, 0:4])
        g = grads[k].reshape(both, chunk_tokens)
        x = normed[k].reshape(chunk_tokens, 2 * cols)
        ones = jnp.ones((8, chunk_tokens), BF16)
        for l in range(layers):
            part = jnp.dot(g[l * feats : (l + 1) * feats], x, preferred_element_type=F32)[
                :, l * cols : (l + 1) * cols
            ]
            if k > 0:
                part = part + enc_sum[l]
            if k < chunks - 1:
                enc_sum[l] = part
            else:
                grad_encoder[l] = part.astype(BF16)
            column = nt(ones, g[l * feats : (l + 1) * feats])[0:1]
            if k > 0:
                column = column + grad_bias[l : l + 1, :]
            grad_bias[l : l + 1, :] = column

    def decoder_grads():
        a = act[...].reshape(tokens, -1)
        e = errors[...].reshape(tokens, 2 * cols)
        first = scale * tn(a[:, 0:feats], e)
        grad_decoder[0] = first[:, 0:cols].astype(BF16)
        grad_decoder[1] = first[:, cols : 2 * cols].astype(BF16)
        second = scale * tn(a[:, feats:both], e)
        grad_decoder[2] = second[:, cols : 2 * cols].astype(BF16)

    stages = (
        pre_matmul, pre_to_z, activate, act_to_core, rebuild, sum_y, sum_xl,
        back_matmul, back_to_z, pre_grad, grads_to_core, encoder_grads,
    )
    order = sorted(
        (STAGE_TIMES[j] + CHUNK_STEP * k, k, j) for k in range(chunks) for j in range(len(stages))
    )
    for _, k, j in order:
        stages[j](k)
        if (k, j) == (chunks - 1, 8):
            decoder_grads()

    for i, ref in pending:
        wait(0, i, ref)


def step(residual, norm_gain, gate_weight, up_weight, down_weight, encoder, encoder_bias, decoder, width):
    layers, local, cols = residual.shape
    feats = encoder.shape[1]
    hid = gate_weight.shape[2]
    chunks, slots, rows = 3, 8, 16
    tokens = slots * rows
    both, wide = layers * feats, layers * cols
    gu_cols = -(-layers * hid // 128) * 128 + layers * hid
    vm = pltpu.VMEM
    scratch = [
        vm((8, layers, 8, 128), F32),
        vm((16, wide), F32),
        vm((8, 16, wide), BF16),
        vm((8 * local, wide), F32),
        vm((chunks, slots, rows, wide), BF16),
        vm((both + layers * hid, wide), BF16),
        vm((both, wide), BF16),
        vm((wide, gu_cols), BF16),
        vm((chunks, slots, rows, both), F32),
        vm((chunks, 4, rows, both), F32),
        vm((chunks, 4, rows, both), F32),
        vm((chunks, 4, rows, both), F32),
        vm((chunks, slots, rows, gu_cols), BF16),
        vm((chunks, 4, rows, gu_cols), BF16),
        vm((chunks, 4, rows, gu_cols), BF16),
        vm((chunks, 4, rows, gu_cols), BF16),
        vm((chunks, slots, rows, both + layers * hid), BF16),
        vm((chunks, slots, rows, wide), BF16),
        vm((chunks, slots, rows, wide), BF16),
        vm((chunks, 8, rows, wide), BF16),
        vm((chunks, slots, rows, wide), BF16),
        vm((chunks, both // slots, tokens), F32),
        vm((chunks, slots, both // slots, tokens), BF16),
        vm((chunks, 4, both // slots, tokens), BF16),
        vm((chunks, 4, both // slots, tokens), BF16),
        vm((chunks, 4, both // slots, tokens), BF16),
        vm((chunks, slots, both // slots, tokens), BF16),
        vm((layers, feats, cols), F32),
        pltpu.SemaphoreType.DMA((2, 2 + chunks * 14)),
    ]
    spec = pl.BlockSpec(memory_space=pltpu.VMEM)
    return pl.pallas_call(
        functools.partial(kernel, width),
        out_shape=(
            jax.ShapeDtypeStruct(encoder.shape, BF16),
            jax.ShapeDtypeStruct(encoder_bias.shape, F32),
            jax.ShapeDtypeStruct(decoder.shape, BF16),
        ),
        in_specs=[spec] * 8,
        out_specs=(spec,) * 3,
        scratch_shapes=scratch,
        compiler_params=pltpu.CompilerParams(
            collective_id=0, has_side_effects=True, vmem_limit_bytes=56 * 2**20
        ),
        name="train_step",
    )(residual, norm_gain, gate_weight, up_weight, down_weight, encoder, encoder_bias, decoder)


def solution(mesh):
    def body(*args):
        return step(*args, width=args[0].shape[2] * mesh.shape["mp"])

    return jax.shard_map(
        body,
        mesh=mesh,
        in_specs=(
            P(None, "feat", "mp"),
            P(None, "mp"),
            P(None, "mp", "feat"),
            P(None, "mp", "feat"),
            P(None, "feat", "mp"),
            P(None, "feat", "mp"),
            P(None, "feat"),
            P(None, "feat", "mp"),
        ),
        out_specs=(P(None, "feat", "mp"), P(None, "feat"), P(None, "feat", "mp")),
        check_vma=False,
    )
```

time: 1200 us -> 137 us (0.11)
  waiting for transfers between devices: 874 us -> 0 us
  blocking collectives: 284 us -> 0 us
  Pallas kernels: 0 us -> 125 us
  matrix products: 15.1 us -> 0 us
  between operations: 14.5 us -> 0.66 us
    unnamed x5 -> x0, waiting for transfers between devices: 555 us -> none
    psum x3 -> x0, waiting for transfers between devices: 319 us -> none  [the longest x1 139 us: body(): lax.psum(back_stack.astype(jnp.bfloat16), 'mp').astype(jnp.float32)]
    all_gather x2 -> x0, blocking collectives: 263 us -> none  [the longest x1 132 us: body(): normed = lax.all_gather(normed_local, 'feat', axis=1, tiled=True)]
    pallas_call x0 -> x1, Pallas kernels: none -> 125 us  [step(): pl.pallas_call(functools.partial(kernel, width), out_shape=(jax.ShapeDtyp...]
    psum x1 -> x0, blocking collectives: 20.4 us -> none  [body(): squares = lax.psum(jnp.sum(values * values, axis=2), 'mp')]
    dot_general x12 -> x0, matrix products: 15.1 us -> none  [the longest x1 2.41 us: body(): jnp.einsum('lth,lhd->tld', picked, down_weight, preferred_element_type=jn...]
  transfers between devices with their start and end apart: 4 -> 0, of which waited for: 4 -> 0; matrix products, arithmetic and copies ran while one was open for 1% -> 0% of each run, Pallas kernels for 0% -> 0%
where the time goes in v1:
time: 137 us
  Pallas kernels  125 us (91%)
  local copies, waits for them, and re-layouts  11.9 us (9%)
    pallas_call x1, Pallas kernels, step(): pl.pallas_call(functools.partial(kernel, width), out_shape=(jax.ShapeDtyp...  125 us
    unnamed x14, local copies, waits for them, and re-layouts  8.24 us
    pallas_call x2, local copies, waits for them, and re-layouts, step(): pl.pallas_call(functools.partial(kernel, width), out_shape=(jax.ShapeDtyp...  3.63 us

profile of v1, /device:TPU:1, one launch (start us, length us, event | category | flops | bytes accessed | tf_op | source)
XLA Modules:
  0.0 137.3 jit_solution(6235533969543070461)
XLA Ops:
  0.6 0.0 copy-start.2
  0.6 1.4 copy.11.residual
  2.0 0.0 copy-start.1
  2.0 1.9 %copy.12.gate_w = bf16[2,288,144]{2,1,0:T(8,128)(2,1)} copy(bf16[2,288,144]{1,2,0:T(8,128)(2,1)} %param.10) | data formatting | bytes 331776 | tf_op args[2]
  3.9 1.8 %copy.13.up_w = bf16[2,288,144]{2,1,0:T(8,128)(2,1)} copy(bf16[2,288,144]{1,2,0:T(8,128)(2,1)} %param.11) | data formatting | bytes 331776 | tf_op args[3]
  5.7 0.0 copy-done.2
  5.7 1.2 copy.14.encoder
  6.9 0.0 copy-done.1
  6.9 1.4 %copy.15.decoder = bf16[3,512,288]{2,1,0:T(8,128)(2,1)} copy(bf16[3,512,288]{1,2,0:T(8,128)(2,1)S(1)} %copy-done.1) | data formatting | bytes 1769472 | tf_op args[7]
  8.3 124.7 %train_step.1 = (bf16[2,512,288]{2,1,0:T(8,128)(2,1)}, f32[2,512]{1,0:T(2,128)}, bf16[3,512,288]{2,1,0:T(8,128)(2,1)}) custom-call(bf16[2,6,288]{2,1,0:T(8,128)(2,1)} %copy.11.residual, f32[2,288]{1,0:T(2,128)} %gain.1, bf16[2,288,144]{2,1,0:T(8,128)(2,1)} %copy.12.gate_w, bf16[2,288,144]{2,1,0:T(8,128)(2,1)} %copy.13.up_w, bf16[2,144,288]{2,1,0:T(8,128)(2,1)} %down_w.1, ...), custom_call_target="tpu_custom_call" | custom-call | tf_op jit(solution)/shard_map/train_step/pallas_call | solution.py:334
  133.0 0.0 copy-start
  133.0 2.3 %copy.16 = bf16[2,512,288]{1,2,0:T(8,128)(2,1)} copy(bf16[2,512,288]{2,1,0:T(8,128)(2,1)} %get-tuple-element.3) | data formatting | bytes 1179648 | tf_op jit(solution)/shard_map/train_step/pallas_call | solution.py:334
  135.3 0.0 copy-done
  135.3 0.0 copy-start.3
  135.3 1.3 copy.17
  136.7 0.0 copy-done.3
  136.7 0.6 copy.19
Async XLA Ops:
  0.6 5.1 %copy-start.2 = (bf16[2,512,288]{1,2,0:T(8,128)(2,1)S(1)}, bf16[2,512,288]{1,2,0:T(8,128)(2,1)}, u32[]{:S(2)}) copy-start(bf16[2,512,288]{1,2,0:T(8,128)(2,1)} %param.13) | copy-start | bytes 1769476
  2.0 4.9 %copy-start.1 = (bf16[3,512,288]{1,2,0:T(8,128)(2,1)S(1)}, bf16[3,512,288]{1,2,0:T(8,128)(2,1)}, u32[]{:S(2)}) copy-start(bf16[3,512,288]{1,2,0:T(8,128)(2,1)} %param.15) | copy-start | bytes 2654212
  133.0 2.3 %copy-start = (bf16[3,512,288]{2,1,0:T(8,128)(2,1)S(1)}, bf16[3,512,288]{2,1,0:T(8,128)(2,1)}, u32[]{:S(2)}) copy-start(bf16[3,512,288]{2,1,0:T(8,128)(2,1)} %get-tuple-element.5) | copy-start | bytes 2654212
  135.3 1.3 copy-start.3

commit v2 on v1

v2 whole, which is shorter than its diff:
```python
import functools
import math

import jax
import jax.numpy as jnp
from jax import lax
from jax.experimental import pallas as pl
from jax.experimental.pallas import tpu as pltpu
from jax.sharding import PartitionSpec as P

MESH = pl.DeviceIdType.MESH
F32 = jnp.float32
BF16 = jnp.bfloat16
sparsity_weight = 0.1

ROWS = (16, 16, 16)
STAGE_TIMES = (0, 1.5, 9, 14, 16, 21, 27, 31, 33, 38, 43, 45)
CHUNK_STEP = 9.0


def nt(a, b):
    return lax.dot_general(a, b, (((1,), (1,)), ((), ())), preferred_element_type=F32)


def kernel(
    width, residual, gain, gate_hbm, up_hbm, down_hbm, encoder, bias, decoder,
    grad_encoder, grad_bias, grad_decoder,
    squares, padded, y_block, own_block, w_dec, w_enc, w_gate, w_down, gate_w, up_w, down_w,
    normed_t, errors_t, enc_sum, sems, local_sems, *per_chunk,
):
    layers, cols, feats = encoder.shape
    local = residual.shape[0]
    hid = gate_w.shape[1]
    chunks, slots = len(ROWS), 8
    both = layers * feats
    tokens = slots * sum(ROWS)
    chunk_tokens = [slots * rows for rows in ROWS]
    first_row = [sum(ROWS[:k]) for k in range(chunks)]
    first_token = [slots * row for row in first_row]
    (
        normed, pre_mine, pre_core, pre_z, pre_recv, gu_mine, gu_core, gu_z, gu_recv, act,
        hidden_all, err_part, err_recv, err_y, errors, back_mine, back_core, back_z, back_recv, grads,
    ) = [per_chunk[i : i + chunks] for i in range(0, len(per_chunk), chunks)]
    scale = 1.0 / math.sqrt(tokens)

    mp = lax.axis_index("mp")
    ft = lax.axis_index("feat")
    zh, core = mp // 2, mp % 2
    xl, yy = ft // 8, ft % 8
    mine = core * 4 + zh

    core_dev = (zh * 2 + 1 - core, ft)
    z_at = [(zh + d) % 4 for d in (1, 2, 3)]
    z_dev = [(z * 2 + core, ft) for z in z_at]
    far_dev = [(z * 2 + 1 - core, ft) for z in z_at]
    xl_at = [(xl + d) % 8 for d in range(1, 8)]
    xl_dev = [(mp, a * 8 + yy) for a in xl_at]
    y_at = [(yy + d) % 8 for d in range(1, 8)]
    y_dev = [(mp, xl * 8 + a) for a in y_at]
    partners = [core_dev] + z_dev + far_dev + xl_dev + y_dev

    pending = []

    def send(i, src, dst, dev):
        pltpu.make_async_remote_copy(
            src_ref=src, dst_ref=dst, send_sem=sems.at[0, i], recv_sem=sems.at[1, i],
            device_id=dev, device_id_type=MESH,
        ).start()

    def wait(side, i, ref):
        pltpu.make_async_copy(ref, ref, sems.at[side, i]).wait()

    barrier = pltpu.get_barrier_semaphore()
    for dev in partners:
        pl.semaphore_signal(barrier, inc=1, device_id=dev, device_id_type=MESH)

    copies = [
        pltpu.make_async_copy(src, dst, local_sems.at[i])
        for i, (src, dst) in enumerate((
            (encoder.at[0], w_enc.at[0:cols, 0:feats]),
            (encoder.at[1], w_enc.at[cols : 2 * cols, feats:both]),
            (decoder.at[0], w_dec.at[0:cols, 0:feats]),
            (decoder.at[1], w_dec.at[cols : 2 * cols, 0:feats]),
            (decoder.at[2], w_dec.at[cols : 2 * cols, feats:both]),
            (gate_hbm, gate_w),
            (up_hbm, up_w),
            (down_hbm, down_w),
        ))
    ]
    for copy in copies:
        copy.start()

    stacked = residual[...].astype(F32)
    values = [stacked[:, l, :] for l in range(layers)]
    sums = [jnp.sum(v * v, axis=1, keepdims=True) for v in values]
    lanes = lax.broadcasted_iota(jnp.int32, (local, 128), 1)
    squares[mp] = jnp.zeros((8, 128), F32)
    squares[mp, 0:local, :] = jnp.where(lanes < 64, sums[0], sums[1])
    padded[...] = jnp.zeros_like(padded)

    pl.semaphore_wait(barrier, len(partners))

    for dev in z_dev + far_dev + [core_dev]:
        send(0, squares.at[mp], squares.at[mp], dev)
    pending.append((0, squares.at[0:7]))

    w_enc[0:cols, feats:both] = jnp.zeros((cols, feats), BF16)
    w_enc[cols : 2 * cols, 0:feats] = jnp.zeros((cols, feats), BF16)
    w_dec[0:cols, feats:both] = jnp.zeros((cols, feats), BF16)
    up_at = 2 * hid
    w_gate[...] = jnp.zeros_like(w_gate)
    w_down[...] = jnp.zeros_like(w_down)

    wait(1, 0, squares.at[0:7])
    total = squares[0]
    for m in range(1, 8):
        total = total + squares[m]
    for l in range(layers):
        inverse = lax.rsqrt(total[0:local, 64 * l : 64 * l + 1] / width + 1e-06)
        padded[l * local : (l + 1) * local, :] = values[l] * inverse * gain[l : l + 1, :]
    y_block[yy] = padded[...].astype(BF16)
    for dev in y_dev:
        send(1, y_block.at[yy], y_block.at[yy], dev)
    pending.append((1, y_block.at[0:7]))

    for copy in copies:
        copy.wait()
    for l in range(layers):
        d, h = slice(l * cols, (l + 1) * cols), slice(l * hid, (l + 1) * hid)
        w_gate[h, d] = gate_w[l]
        w_gate[up_at + l * hid : up_at + (l + 1) * hid, d] = up_w[l]
        w_down[h, d] = down_w[l]

    wait(1, 1, y_block.at[0:7])
    for s in range(8):
        arrived = y_block[s].astype(F32)
        for l in range(layers):
            own_block[s * local : (s + 1) * local, l * cols : (l + 1) * cols] = arrived[
                l * local : (l + 1) * local, :
            ]
    for k in range(chunks):
        normed[k][xl] = own_block[first_row[k] : first_row[k] + ROWS[k], :].astype(BF16)
        for dev in xl_dev:
            send(2 + k, normed[k].at[xl], normed[k].at[xl], dev)
        pending.append((2 + k, normed[k].at[0:7]))

    def slot(kind, k):
        return 2 + chunks * (1 + kind) + k

    def pre_matmul(k):
        wait(1, 2 + k, normed[k].at[0:7])
        x = normed[k][...].reshape(chunk_tokens[k], 2 * cols)
        pre_mine[k][...] = jnp.dot(x, w_enc[...], preferred_element_type=F32).reshape(slots, ROWS[k], both)
        send(slot(0, k), pre_mine[k].at[pl.ds((1 - core) * 4, 4)], pre_core[k], core_dev)
        pending.append((slot(0, k), pre_core[k]))
        gu_mine[k][...] = nt(x, w_gate[...]).astype(BF16).reshape(slots, ROWS[k], -1)
        send(slot(1, k), gu_mine[k].at[pl.ds((1 - core) * 4, 4)], gu_core[k], core_dev)
        pending.append((slot(1, k), gu_core[k]))

    def pre_to_z(k):
        wait(1, slot(0, k), pre_core[k])
        for z, dev in zip(z_at, z_dev):
            pre_z[k][z] = pre_mine[k][core * 4 + z] + pre_core[k][z]
            send(slot(2, k), pre_z[k].at[z], pre_recv[k].at[zh], dev)
        pending.append((slot(2, k), pre_z[k].at[0:3]))
        pre_recv[k][zh] = pre_mine[k][mine] + pre_core[k][zh]
        wait(1, slot(1, k), gu_core[k])
        for z, dev in zip(z_at, z_dev):
            gu_z[k][z] = (gu_mine[k][core * 4 + z].astype(F32) + gu_core[k][z].astype(F32)).astype(BF16)
            send(slot(3, k), gu_z[k].at[z], gu_recv[k].at[zh], dev)
        pending.append((slot(3, k), gu_z[k].at[0:3]))
        gu_recv[k][zh] = (gu_mine[k][mine].astype(F32) + gu_core[k][zh].astype(F32)).astype(BF16)
        normed_t[:, first_token[k] : first_token[k] + chunk_tokens[k]] = normed[k][...].reshape(chunk_tokens[k], 2 * cols).T

    def activate(k):
        wait(1, slot(2, k), pre_recv[k].at[0:3])
        total = pre_recv[k][0] + pre_recv[k][1] + pre_recv[k][2] + pre_recv[k][3]
        for l in range(layers):
            act[k][mine, :, l * feats : (l + 1) * feats] = jnp.maximum(
                total[:, l * feats : (l + 1) * feats] + bias[l : l + 1, :], 0.0
            ).astype(BF16)
        for dev in z_dev:
            send(slot(4, k), act[k].at[mine], act[k].at[mine], dev)
        pending.append((slot(4, k), act[k].at[0:3]))
        wait(1, slot(3, k), gu_recv[k].at[0:3])
        gu = gu_recv[k][0].astype(F32)
        for z in range(1, 4):
            gu = gu + gu_recv[k][z].astype(F32)
        hidden = jax.nn.gelu(gu[:, 0 : 2 * hid], approximate=True) * gu[:, up_at : up_at + 2 * hid]
        hidden_all[k][mine] = hidden.astype(BF16)
        for dev in z_dev:
            send(slot(13, k), hidden_all[k].at[mine], hidden_all[k].at[mine], dev)
        pending.append((slot(13, k), hidden_all[k].at[0:3]))

    def act_to_core(k):
        wait(1, slot(4, k), act[k].at[0:3])
        half = act[k].at[pl.ds(core * 4, 4)]
        send(slot(5, k), half, half, core_dev)
        pending.append((slot(5, k), act[k].at[0:4]))
        wait(1, slot(13, k), hidden_all[k].at[0:3])
        half = hidden_all[k].at[pl.ds(core * 4, 4)]
        send(slot(14, k), half, half, core_dev)
        pending.append((slot(14, k), hidden_all[k].at[0:4]))

    def rebuild(k):
        wait(1, slot(5, k), act[k].at[0:4])
        wait(1, slot(14, k), hidden_all[k].at[0:4])
        part = nt(act[k][...].reshape(chunk_tokens[k], both), w_dec[...]) - jnp.dot(
            hidden_all[k][...].reshape(chunk_tokens[k], 2 * hid), w_down[...], preferred_element_type=F32
        )
        err_part[k][...] = part.astype(BF16).reshape(slots, ROWS[k], -1)
        for s, dev in zip(xl_at, xl_dev):
            send(slot(6, k), err_part[k].at[s], err_recv[k].at[xl], dev)
        pending.append((slot(6, k), err_part[k].at[0:7]))
        err_recv[k][xl] = err_part[k][xl]

    def sum_first(k):
        wait(1, slot(6, k), err_recv[k].at[0:7])
        total = err_recv[k][0].astype(F32)
        for s in range(1, 8):
            total = total + err_recv[k][s].astype(F32)
        err_y[k][yy] = total.astype(BF16)
        for dev in y_dev:
            send(slot(7, k), err_y[k].at[yy], err_y[k].at[yy], dev)
        pending.append((slot(7, k), err_y[k].at[0:7]))

    def sum_y(k):
        wait(1, slot(7, k), err_y[k].at[0:7])
        total = err_y[k][0].astype(F32)
        for s in range(1, 8):
            total = total + err_y[k][s].astype(F32)
        errors[k][xl] = total.astype(BF16)
        for dev in xl_dev:
            send(slot(8, k), errors[k].at[xl], errors[k].at[xl], dev)
        pending.append((slot(8, k), errors[k].at[0:7]))

    def back_matmul(k):
        wait(1, slot(8, k), errors[k].at[0:7])
        e = errors[k][...].reshape(chunk_tokens[k], 2 * cols)
        back = jnp.dot(e, w_dec[...], preferred_element_type=F32)
        back_mine[k][...] = back.astype(BF16).reshape(slots, ROWS[k], both)
        send(slot(9, k), back_mine[k].at[pl.ds((1 - core) * 4, 4)], back_core[k], core_dev)
        pending.append((slot(9, k), back_core[k]))

    def back_to_z(k):
        wait(1, slot(9, k), back_core[k])
        for z, dev in zip(z_at, z_dev):
            back_z[k][z] = (
                back_mine[k][core * 4 + z].astype(F32) + back_core[k][z].astype(F32)
            ).astype(BF16)
            send(slot(10, k), back_z[k].at[z], back_recv[k].at[zh], dev)
        pending.append((slot(10, k), back_z[k].at[0:3]))
        back_recv[k][zh] = (
            back_mine[k][mine].astype(F32) + back_core[k][zh].astype(F32)
        ).astype(BF16)
        errors_t[:, first_token[k] : first_token[k] + chunk_tokens[k]] = errors[k][...].reshape(chunk_tokens[k], 2 * cols).T

    def pre_grad(k):
        wait(1, slot(10, k), back_recv[k].at[0:3])
        total = back_recv[k][0].astype(F32)
        for z in range(1, 4):
            total = total + back_recv[k][z].astype(F32)
        grads[k][mine] = jnp.where(
            act[k][mine].astype(F32) > 0, scale * (total + sparsity_weight), 0.0
        ).astype(BF16)
        for dev in z_dev:
            send(slot(11, k), grads[k].at[mine], grads[k].at[mine], dev)
        pending.append((slot(11, k), grads[k].at[0:3]))

    def grads_to_core(k):
        wait(1, slot(11, k), grads[k].at[0:3])
        half = grads[k].at[pl.ds(core * 4, 4)]
        send(slot(12, k), half, half, core_dev)
        pending.append((slot(12, k), grads[k].at[0:4]))

    def encoder_grads(k):
        wait(1, slot(12, k), grads[k].at[0:4])
        g = grads[k][...].reshape(chunk_tokens[k], both)
        ones = jnp.ones((8, chunk_tokens[k]), BF16)
        for l in range(layers):
            g_layer = g[:, l * feats : (l + 1) * feats]
            x_t = normed_t[l * cols : (l + 1) * cols, first_token[k] : first_token[k] + chunk_tokens[k]]
            part = jnp.dot(x_t, g_layer, preferred_element_type=F32)
            if k > 0:
                part = part + enc_sum[l]
            if k < chunks - 1:
                enc_sum[l] = part
            else:
                grad_encoder[l] = part.astype(BF16)
            column = jnp.dot(ones, g_layer, preferred_element_type=F32)[0:1]
            if k > 0:
                column = column + grad_bias[l : l + 1, :]
            grad_bias[l : l + 1, :] = column

    def decoder_grads():
        first = second = None
        for k in range(chunks):
            a = act[k][...].reshape(chunk_tokens[k], both)
            e = errors_t[:, first_token[k] : first_token[k] + chunk_tokens[k]]
            one = jnp.dot(e, a[:, 0:feats], preferred_element_type=F32)
            two = jnp.dot(e[cols : 2 * cols], a[:, feats:both], preferred_element_type=F32)
            first, second = (one, two) if k == 0 else (first + one, second + two)
        grad_decoder[0] = (first[0:cols] * scale).astype(BF16)
        grad_decoder[1] = (first[cols : 2 * cols] * scale).astype(BF16)
        grad_decoder[2] = (second * scale).astype(BF16)

    stages = (
        pre_matmul, pre_to_z, activate, act_to_core, rebuild, sum_first, sum_y,
        back_matmul, back_to_z, pre_grad, grads_to_core, encoder_grads,
    )
    order = sorted(
        (STAGE_TIMES[j] + CHUNK_STEP * k, k, j) for k in range(chunks) for j in range(len(stages))
    )
    for _, k, j in order:
        stages[j](k)
        if (k, j) == (chunks - 1, 8):
            decoder_grads()

    for i, ref in pending:
        wait(0, i, ref)


def step(residual, norm_gain, gate_weight, up_weight, down_weight, encoder, encoder_bias, decoder, width):
    layers, local, cols = residual.shape
    feats = encoder.shape[1]
    hid = gate_weight.shape[2]
    chunks, slots = len(ROWS), 8
    tokens = slots * sum(ROWS)
    both, wide, hidden, gate_up = layers * feats, layers * cols, layers * hid, 2 * layers * hid
    vm = pltpu.VMEM
    scratch = [
        vm((8, 8, 128), F32),
        vm((16, cols), F32),
        vm((8, 16, cols), BF16),
        vm((8 * local, wide), F32),
        vm((wide, both), BF16),
        vm((wide, both), BF16),
        vm((gate_up, wide), BF16),
        vm((hidden, wide), BF16),
        vm((layers, hid, cols), BF16),
        vm((layers, hid, cols), BF16),
        vm((layers, hid, cols), BF16),
        vm((wide, tokens), BF16),
        vm((wide, tokens), BF16),
        vm((layers, cols, feats), F32),
        pltpu.SemaphoreType.DMA((2, 2 + chunks * 16)),
        pltpu.SemaphoreType.DMA((8,)),
    ]
    for lead, last, dtype in (
        (slots, wide, BF16),
        (slots, both, F32), (4, both, F32), (4, both, F32), (4, both, F32),
        (slots, gate_up, BF16), (4, gate_up, BF16), (4, gate_up, BF16), (4, gate_up, BF16),
        (slots, both, BF16), (slots, hidden, BF16),
        (slots, wide, BF16), (slots, wide, BF16), (8, wide, BF16), (slots, wide, BF16),
        (slots, both, BF16), (4, both, BF16), (4, both, BF16), (4, both, BF16), (slots, both, BF16),
    ):
        scratch += [vm((lead, rows, last), dtype) for rows in ROWS]
    spec = pl.BlockSpec(memory_space=pltpu.VMEM)
    anywhere = pl.BlockSpec(memory_space=pl.ANY)
    grad_encoder, grad_bias, grad_decoder = pl.pallas_call(
        functools.partial(kernel, width),
        out_shape=(
            jax.ShapeDtypeStruct((layers, cols, feats), BF16),
            jax.ShapeDtypeStruct(encoder_bias.shape, F32),
            jax.ShapeDtypeStruct((decoder.shape[0], cols, feats), BF16),
        ),
        in_specs=[spec, spec, anywhere, anywhere, anywhere, anywhere, spec, anywhere],
        out_specs=(spec,) * 3,
        scratch_shapes=scratch,
        compiler_params=pltpu.CompilerParams(
            collective_id=0, has_side_effects=True, vmem_limit_bytes=56 * 2**20
        ),
        name="train_step",
    )(
        residual.swapaxes(0, 1), norm_gain, gate_weight.swapaxes(1, 2), up_weight.swapaxes(1, 2),
        down_weight, encoder.swapaxes(1, 2), encoder_bias, decoder.swapaxes(1, 2),
    )
    return grad_encoder.swapaxes(1, 2), grad_bias, grad_decoder.swapaxes(1, 2)


def solution(mesh):
    def body(*args):
        return step(*args, width=args[0].shape[2] * mesh.shape["mp"])

    return jax.shard_map(
        body,
        mesh=mesh,
        in_specs=(
            P(None, "feat", "mp"),
            P(None, "mp"),
            P(None, "mp", "feat"),
            P(None, "mp", "feat"),
            P(None, "feat", "mp"),
            P(None, "feat", "mp"),
            P(None, "feat"),
            P(None, "feat", "mp"),
        ),
        out_specs=(P(None, "feat", "mp"), P(None, "feat"), P(None, "feat", "mp")),
        check_vma=False,
    )
```

time: 137 us -> 120 us (0.88)
  Pallas kernels: 125 us -> 116 us
  local copies, waits for them, and re-layouts: 11.9 us -> 3.51 us
    pallas_call x1, Pallas kernels: 125 us -> 116 us  [step(): pl.pallas_call(functools.partial(kernel, width), out_shape=(jax.ShapeDtyp...]
    unnamed x14 -> x7, local copies, waits for them, and re-layouts: 8.24 us -> 3.51 us
    pallas_call x2 -> x0, local copies, waits for them, and re-layouts: 3.63 us -> none  [step(): pl.pallas_call(functools.partial(kernel, width), out_shape=(jax.ShapeDtyp...]
where the time goes in v2:
time: 120 us
  Pallas kernels  116 us (97%)
  local copies, waits for them, and re-layouts  3.51 us (3%)
    pallas_call x1, Pallas kernels, step(): pl.pallas_call(functools.partial(kernel, width), out_shape=(jax.ShapeDtyp...  116 us
    unnamed x7, local copies, waits for them, and re-layouts  3.51 us

profile of v2, /device:TPU:1, one launch (start us, length us, event | category | flops | bytes accessed | tf_op | source)
XLA Modules:
  0.0 119.7 jit_solution(16881396736381861664)
XLA Ops:
  0.6 115.6 %train_step.1 = (bf16[2,288,512]{2,1,0:T(8,128)(2,1)}, f32[2,512]{1,0:T(2,128)}, bf16[3,288,512]{2,1,0:T(8,128)(2,1)}) custom-call(bf16[6,2,288]{2,1,0:T(2,128)(2,1)} %bitcast.13, f32[2,288]{1,0:T(2,128)} %gain.1, bf16[2,144,288]{2,1,0:T(8,128)(2,1)} %bitcast.11, bf16[2,144,288]{2,1,0:T(8,128)(2,1)} %bitcast.12, bf16[2,144,288]{2,1,0:T(8,128)(2,1)} %down_hbm.1, ...), custom_call_target="tpu_custom_call" | custom-call | tf_op jit(solution)/shard_map/train_step/pallas_call | solution.py:360
  116.2 0.0 copy-start
  116.2 0.0 copy-start.1
  116.2 2.0 %copy.14 = bf16[2,512,288]{1,2,0:T(8,128)(2,1)} copy(bf16[2,512,288]{1,2,0:T(8,128)(2,1)} %bitcast.9) | data formatting | bytes 1179648
  118.2 0.0 copy-done.1
  118.2 0.6 copy.15
  118.8 0.0 copy-done
  118.8 0.9 copy.16
Async XLA Ops:
  116.2 2.6 %copy-start = (bf16[3,288,512]{2,1,0:T(8,128)(2,1)S(1)}, bf16[3,288,512]{2,1,0:T(8,128)(2,1)}, u32[]{:S(2)}) copy-start(bf16[3,288,512]{2,1,0:T(8,128)(2,1)} %get-tuple-element.8) | copy-start | bytes 2654212
  116.2 2.0 %copy-start.1 = (f32[2,512]{1,0:T(2,128)S(1)}, f32[2,512]{1,0:T(2,128)}, u32[]{:S(2)}) copy-start(f32[2,512]{1,0:T(2,128)} %get-tuple-element.13) | copy-start | bytes 12292

commit v3 on v2

--- a/solution.py
+++ b/solution.py
@@ -25,7 +25,7 @@
 def kernel(
     width, residual, gain, gate_hbm, up_hbm, down_hbm, encoder, bias, decoder,
     grad_encoder, grad_bias, grad_decoder,
-    squares, padded, y_block, own_block, w_dec, w_enc, w_gate, w_down, gate_w, up_w, down_w,
+    squares, padded, plane_block, own_block, w_dec, w_enc, w_gate, w_down, gate_w, up_w, down_w,
     normed_t, errors_t, enc_sum, sems, local_sems, *per_chunk,
 ):
     layers, cols, feats = encoder.shape
@@ -47,17 +47,21 @@
     ft = lax.axis_index("feat")
     zh, core = mp // 2, mp % 2
     xl, yy = ft // 8, ft % 8
+    xx, plane = xl % 4, xl // 4 * 8 + yy
     mine = core * 4 + zh
 
     core_dev = (zh * 2 + 1 - core, ft)
-    z_at = [(zh + d) % 4 for d in (1, 2, 3)]
+    z_at = [(zh + d) % 4 for d in (2, 1, 3)]
     z_dev = [(z * 2 + core, ft) for z in z_at]
     far_dev = [(z * 2 + 1 - core, ft) for z in z_at]
     xl_at = [(xl + d) % 8 for d in range(1, 8)]
     xl_dev = [(mp, a * 8 + yy) for a in xl_at]
-    y_at = [(yy + d) % 8 for d in range(1, 8)]
-    y_dev = [(mp, xl * 8 + a) for a in y_at]
-    partners = [core_dev] + z_dev + far_dev + xl_dev + y_dev
+    x_dev = [(mp, (xl // 4 * 4 + (xx + d) % 4) * 8 + yy) for d in (2, 1, 3)]
+    y_dev = [(mp, xl * 8 + (yy + d) % 8) for d in (4, 3, 5, 2, 6, 1, 7)]
+    plane_at = [(plane + d) % 16 for d in range(1, 16)]
+    plane_dev = [(mp, (a // 8 * 4 + xx) * 8 + a % 8) for a in plane_at]
+    diagonal_dev = [(mp, ((1 - xl // 4) * 4 + (xx + d) % 4) * 8 + yy) for d in (1, 2, 3)]
+    partners = [core_dev] + z_dev + far_dev + x_dev + diagonal_dev + plane_dev
 
     pending = []
 
@@ -118,10 +122,10 @@
     for l in range(layers):
         inverse = lax.rsqrt(total[0:local, 64 * l : 64 * l + 1] / width + 1e-06)
         padded[l * local : (l + 1) * local, :] = values[l] * inverse * gain[l : l + 1, :]
-    y_block[yy] = padded[...].astype(BF16)
-    for dev in y_dev:
-        send(1, y_block.at[yy], y_block.at[yy], dev)
-    pending.append((1, y_block.at[0:7]))
+    plane_block[plane] = padded[...].astype(BF16)
+    for dev in plane_dev:
+        send(1, plane_block.at[plane], plane_block.at[plane], dev)
+    pending.append((1, plane_block.at[0:15]))
 
     for copy in copies:
         copy.wait()
@@ -131,24 +135,24 @@
         w_gate[up_at + l * hid : up_at + (l + 1) * hid, d] = up_w[l]
         w_down[h, d] = down_w[l]
 
-    wait(1, 1, y_block.at[0:7])
-    for s in range(8):
-        arrived = y_block[s].astype(F32)
+    wait(1, 1, plane_block.at[0:15])
+    for s in range(16):
+        arrived = plane_block[s].astype(F32)
         for l in range(layers):
             own_block[s * local : (s + 1) * local, l * cols : (l + 1) * cols] = arrived[
                 l * local : (l + 1) * local, :
             ]
     for k in range(chunks):
-        normed[k][xl] = own_block[first_row[k] : first_row[k] + ROWS[k], :].astype(BF16)
-        for dev in xl_dev:
-            send(2 + k, normed[k].at[xl], normed[k].at[xl], dev)
-        pending.append((2 + k, normed[k].at[0:7]))
+        normed[k][xx] = own_block[2 * first_row[k] : 2 * (first_row[k] + ROWS[k]), :].astype(BF16)
+        for dev in x_dev:
+            send(2 + k, normed[k].at[xx], normed[k].at[xx], dev)
+        pending.append((2 + k, normed[k].at[0:3]))
 
     def slot(kind, k):
         return 2 + chunks * (1 + kind) + k
 
     def pre_matmul(k):
-        wait(1, 2 + k, normed[k].at[0:7])
+        wait(1, 2 + k, normed[k].at[0:3])
         x = normed[k][...].reshape(chunk_tokens[k], 2 * cols)
         pre_mine[k][...] = jnp.dot(x, w_enc[...], preferred_element_type=F32).reshape(slots, ROWS[k], both)
         send(slot(0, k), pre_mine[k].at[pl.ds((1 - core) * 4, 4)], pre_core[k], core_dev)
@@ -320,6 +324,16 @@
         wait(0, i, ref)
 
 
+def hand_over(*refs):
+    copies = [
+        pltpu.make_async_copy(refs[i], refs[3 + i], refs[6].at[i]) for i in range(3)
+    ]
+    for copy in copies:
+        copy.start()
+    for copy in copies:
+        copy.wait()
+
+
 def step(residual, norm_gain, gate_weight, up_weight, down_weight, encoder, encoder_bias, decoder, width):
     layers, local, cols = residual.shape
     feats = encoder.shape[1]
@@ -331,8 +345,8 @@
     scratch = [
         vm((8, 8, 128), F32),
         vm((16, cols), F32),
-        vm((8, 16, cols), BF16),
-        vm((8 * local, wide), F32),
+        vm((16, 16, cols), BF16),
+        vm((16 * local, wide), F32),
         vm((wide, both), BF16),
         vm((wide, both), BF16),
         vm((gate_up, wide), BF16),
@@ -346,8 +360,8 @@
         pltpu.SemaphoreType.DMA((2, 2 + chunks * 16)),
         pltpu.SemaphoreType.DMA((8,)),
     ]
+    scratch += [vm((4, 2 * rows, wide), BF16) for rows in ROWS]
     for lead, last, dtype in (
-        (slots, wide, BF16),
         (slots, both, F32), (4, both, F32), (4, both, F32), (4, both, F32),
         (slots, gate_up, BF16), (4, gate_up, BF16), (4, gate_up, BF16), (4, gate_up, BF16),
         (slots, both, BF16), (slots, hidden, BF16),
@@ -375,6 +389,15 @@
         residual.swapaxes(0, 1), norm_gain, gate_weight.swapaxes(1, 2), up_weight.swapaxes(1, 2),
         down_weight, encoder.swapaxes(1, 2), encoder_bias, decoder.swapaxes(1, 2),
     )
+    results = (grad_encoder, grad_bias, grad_decoder)
+    grad_encoder, grad_bias, grad_decoder = pl.pallas_call(
+        hand_over,
+        out_shape=tuple(jax.ShapeDtypeStruct(r.shape, r.dtype) for r in results),
+        in_specs=[anywhere] * 3,
+        out_specs=(anywhere,) * 3,
+        scratch_shapes=[pltpu.SemaphoreType.DMA((3,))],
+        name="results",
+    )(*results)
     return grad_encoder.swapaxes(1, 2), grad_bias, grad_decoder.swapaxes(1, 2)
 
 

time: 120 us -> 161 us (1.34)
  Pallas kernels: 116 us -> 161 us
  local copies, waits for them, and re-layouts: 3.51 us -> 0 us
    pallas_call x0 -> x1, Pallas kernels: none -> 45.9 us  [step(): pl.pallas_call(hand_over, out_shape=tuple((jax.ShapeDtypeStruct(r.shape,...]
    unnamed x7 -> x0, local copies, waits for them, and re-layouts: 3.51 us -> none
where the time goes in v3:
time: 161 us
  Pallas kernels  161 us (100%)
    pallas_call x1, Pallas kernels, step(): pl.pallas_call(functools.partial(kernel, width), out_shape=(jax.ShapeDtyp...  115 us
    pallas_call x1, Pallas kernels, step(): pl.pallas_call(hand_over, out_shape=tuple((jax.ShapeDtypeStruct(r.shape,...  45.9 us

profile of v3, /device:TPU:1, one launch (start us, length us, event | category | flops | bytes accessed | tf_op | source)
XLA Modules:
  0.0 161.3 jit_solution(15948679552048030704)
XLA Ops:
  0.6 114.7 %train_step.1 = (bf16[2,288,512]{2,1,0:T(8,128)(2,1)}, f32[2,512]{1,0:T(2,128)}, bf16[3,288,512]{2,1,0:T(8,128)(2,1)}) custom-call(bf16[6,2,288]{2,1,0:T(2,128)(2,1)} %bitcast.11, f32[2,288]{1,0:T(2,128)} %gain.1, bf16[2,144,288]{2,1,0:T(8,128)(2,1)} %bitcast.9, bf16[2,144,288]{2,1,0:T(8,128)(2,1)} %bitcast.10, bf16[2,144,288]{2,1,0:T(8,128)(2,1)} %down_hbm.1, ...), custom_call_target="tpu_custom_call" | custom-call | tf_op jit(solution)/shard_map/train_step/pallas_call | solution.py:374
  115.4 45.9 %results.1 = (bf16[2,288,512]{2,1,0:T(8,128)(2,1)}, f32[2,512]{1,0:T(2,128)}, bf16[3,288,512]{2,1,0:T(8,128)(2,1)}) custom-call(bf16[2,288,512]{2,1,0:T(8,128)(2,1)} %get-tuple-element.9.refs_0_, f32[2,512]{1,0:T(2,128)} %get-tuple-element.10.refs_1_, bf16[3,288,512]{2,1,0:T(8,128)(2,1)} %get-tuple-element.11.refs_2_), custom_call_target="tpu_custom_call" | custom-call | tf_op jit(solution)/shard_map/results/pallas_call | solution.py:393

commit v4 on v3

--- a/solution.py
+++ b/solution.py
@@ -39,7 +39,7 @@
     first_token = [slots * row for row in first_row]
     (
         normed, pre_mine, pre_core, pre_z, pre_recv, gu_mine, gu_core, gu_z, gu_recv, act,
-        hidden_all, err_part, err_recv, err_y, errors, back_mine, back_core, back_z, back_recv, grads,
+        hidden_all, err_part, err_recv, err_xl, errors, back_mine, back_core, back_z, back_recv, grads,
     ) = [per_chunk[i : i + chunks] for i in range(0, len(per_chunk), chunks)]
     scale = 1.0 / math.sqrt(tokens)
 
@@ -57,7 +57,8 @@
     xl_at = [(xl + d) % 8 for d in range(1, 8)]
     xl_dev = [(mp, a * 8 + yy) for a in xl_at]
     x_dev = [(mp, (xl // 4 * 4 + (xx + d) % 4) * 8 + yy) for d in (2, 1, 3)]
-    y_dev = [(mp, xl * 8 + (yy + d) % 8) for d in (4, 3, 5, 2, 6, 1, 7)]
+    y_at = [(yy + d) % 8 for d in (4, 3, 5, 2, 6, 1, 7)]
+    y_dev = [(mp, xl * 8 + a) for a in y_at]
     plane_at = [(plane + d) % 16 for d in range(1, 16)]
     plane_dev = [(mp, (a // 8 * 4 + xx) * 8 + a % 8) for a in plane_at]
     diagonal_dev = [(mp, ((1 - xl // 4) * 4 + (xx + d) % 4) * 8 + yy) for d in (1, 2, 3)]
@@ -213,29 +214,29 @@
             hidden_all[k][...].reshape(chunk_tokens[k], 2 * hid), w_down[...], preferred_element_type=F32
         )
         err_part[k][...] = part.astype(BF16).reshape(slots, ROWS[k], -1)
-        for s, dev in zip(xl_at, xl_dev):
-            send(slot(6, k), err_part[k].at[s], err_recv[k].at[xl], dev)
+        for s, dev in zip(y_at, y_dev):
+            send(slot(6, k), err_part[k].at[s], err_recv[k].at[yy], dev)
         pending.append((slot(6, k), err_part[k].at[0:7]))
-        err_recv[k][xl] = err_part[k][xl]
-
-    def sum_first(k):
+        err_recv[k][yy] = err_part[k][yy]
+
+    def sum_y(k):
         wait(1, slot(6, k), err_recv[k].at[0:7])
         total = err_recv[k][0].astype(F32)
         for s in range(1, 8):
             total = total + err_recv[k][s].astype(F32)
-        err_y[k][yy] = total.astype(BF16)
+        err_xl[k][xl] = total.astype(BF16)
+        for dev in xl_dev:
+            send(slot(7, k), err_xl[k].at[xl], err_xl[k].at[xl], dev)
+        pending.append((slot(7, k), err_xl[k].at[0:7]))
+
+    def sum_xl(k):
+        wait(1, slot(7, k), err_xl[k].at[0:7])
+        total = err_xl[k][0].astype(F32)
+        for s in range(1, 8):
+            total = total + err_xl[k][s].astype(F32)
+        errors[k][yy] = total.astype(BF16)
         for dev in y_dev:
-            send(slot(7, k), err_y[k].at[yy], err_y[k].at[yy], dev)
-        pending.append((slot(7, k), err_y[k].at[0:7]))
-
-    def sum_y(k):
-        wait(1, slot(7, k), err_y[k].at[0:7])
-        total = err_y[k][0].astype(F32)
-        for s in range(1, 8):
-            total = total + err_y[k][s].astype(F32)
-        errors[k][xl] = total.astype(BF16)
-        for dev in xl_dev:
-            send(slot(8, k), errors[k].at[xl], errors[k].at[xl], dev)
+            send(slot(8, k), errors[k].at[yy], errors[k].at[yy], dev)
         pending.append((slot(8, k), errors[k].at[0:7]))
 
     def back_matmul(k):
@@ -309,7 +310,7 @@
         grad_decoder[2] = (second * scale).astype(BF16)
 
     stages = (
-        pre_matmul, pre_to_z, activate, act_to_core, rebuild, sum_first, sum_y,
+        pre_matmul, pre_to_z, activate, act_to_core, rebuild, sum_y, sum_xl,
         back_matmul, back_to_z, pre_grad, grads_to_core, encoder_grads,
     )
     order = sorted(
@@ -322,16 +323,6 @@
 
     for i, ref in pending:
         wait(0, i, ref)
-
-
-def hand_over(*refs):
-    copies = [
-        pltpu.make_async_copy(refs[i], refs[3 + i], refs[6].at[i]) for i in range(3)
-    ]
-    for copy in copies:
-        copy.start()
-    for copy in copies:
-        copy.wait()
 
 
 def step(residual, norm_gain, gate_weight, up_weight, down_weight, encoder, encoder_bias, decoder, width):
@@ -389,15 +380,6 @@
         residual.swapaxes(0, 1), norm_gain, gate_weight.swapaxes(1, 2), up_weight.swapaxes(1, 2),
         down_weight, encoder.swapaxes(1, 2), encoder_bias, decoder.swapaxes(1, 2),
     )
-    results = (grad_encoder, grad_bias, grad_decoder)
-    grad_encoder, grad_bias, grad_decoder = pl.pallas_call(
-        hand_over,
-        out_shape=tuple(jax.ShapeDtypeStruct(r.shape, r.dtype) for r in results),
-        in_specs=[anywhere] * 3,
-        out_specs=(anywhere,) * 3,
-        scratch_shapes=[pltpu.SemaphoreType.DMA((3,))],
-        name="results",
-    )(*results)
     return grad_encoder.swapaxes(1, 2), grad_bias, grad_decoder.swapaxes(1, 2)
 
 

time: 161 us -> 120 us (0.75)
  Pallas kernels: 161 us -> 116 us
  local copies, waits for them, and re-layouts: 0 us -> 3.51 us
    pallas_call x1 -> x0, Pallas kernels: 45.9 us -> none  [step(): pl.pallas_call(hand_over, out_shape=tuple((jax.ShapeDtypeStruct(r.shape,...]
    unnamed x0 -> x7, local copies, waits for them, and re-layouts: none -> 3.51 us
where the time goes in v4:
time: 120 us
  Pallas kernels  116 us (97%)
  local copies, waits for them, and re-layouts  3.51 us (3%)
    pallas_call x1, Pallas kernels, step(): pl.pallas_call(functools.partial(kernel, width), out_shape=(jax.ShapeDtyp...  116 us
    unnamed x7, local copies, waits for them, and re-layouts  3.51 us

profile of v4, /device:TPU:1, one launch (start us, length us, event | category | flops | bytes accessed | tf_op | source)
XLA Modules:
  0.0 120.2 jit_solution(9428176435426864537)
XLA Ops:
  0.6 116.0 %train_step.1 = (bf16[2,288,512]{2,1,0:T(8,128)(2,1)}, f32[2,512]{1,0:T(2,128)}, bf16[3,288,512]{2,1,0:T(8,128)(2,1)}) custom-call(bf16[6,2,288]{2,1,0:T(2,128)(2,1)} %bitcast.13, f32[2,288]{1,0:T(2,128)} %gain.1, bf16[2,144,288]{2,1,0:T(8,128)(2,1)} %bitcast.11, bf16[2,144,288]{2,1,0:T(8,128)(2,1)} %bitcast.12, bf16[2,144,288]{2,1,0:T(8,128)(2,1)} %down_hbm.1, ...), custom_call_target="tpu_custom_call" | custom-call | tf_op jit(solution)/shard_map/train_step/pallas_call | solution.py:365
  116.7 0.0 copy-start
  116.7 0.0 copy-start.1
  116.7 2.0 %copy.14 = bf16[2,512,288]{1,2,0:T(8,128)(2,1)} copy(bf16[2,512,288]{1,2,0:T(8,128)(2,1)} %bitcast.9) | data formatting | bytes 1179648
  118.7 0.0 copy-done.1
  118.7 0.6 copy.15
  119.3 0.0 copy-done
  119.3 0.9 copy.16
Async XLA Ops:
  116.7 2.6 %copy-start = (bf16[3,288,512]{2,1,0:T(8,128)(2,1)S(1)}, bf16[3,288,512]{2,1,0:T(8,128)(2,1)}, u32[]{:S(2)}) copy-start(bf16[3,288,512]{2,1,0:T(8,128)(2,1)} %get-tuple-element.8) | copy-start | bytes 2654212
  116.7 2.0 %copy-start.1 = (f32[2,512]{1,0:T(2,128)S(1)}, f32[2,512]{1,0:T(2,128)}, u32[]{:S(2)}) copy-start(f32[2,512]{1,0:T(2,128)} %get-tuple-element.13) | copy-start | bytes 12292
